TPU v7x, 512 devices: a whole 4x4x16 slice. The times are simulated.
512 devices in a mesh: lab: 32 (over z_lo, y, core), img: 16 (over x, z_hi).
Axes of the slice: x: 4, y: 4, z: 16 (z_hi: 4, z_lo: 4; z = z_hi * 4 + z_lo), core: 2. Of those that a mesh axis runs over, the one named last changes fastest.
Arguments:
- queries: bfloat16 [32768, 512], P('lab'), may hold values from -12 to 12
- keys: bfloat16 [16, 576, 512], P('img', 'lab'), may hold values from -5 to 5
- values: bfloat16 [16, 576, 512], P('img', 'lab'), may hold values from -6 to 6
- grad_out: bfloat16 [16, 32768, 512], P('img', 'lab'), may hold values from -6 to 6
- block_mask: int32 [256, 16], P('lab', 'img'), may hold values from 0 to 1, as said below
Outputs:
- grad_queries: bfloat16 [32768, 512], P(('lab', 'img'))
- grad_keys: bfloat16 [16, 576, 512], P('img', 'lab')
- grad_values: bfloat16 [16, 576, 512], P('img', 'lab')
Inputs may be any that keep to these rules, and one draw needn't show every extreme that they name: `block_mask`: each label block has its own density of images that it reads.
All inputs are finite; a program needn't handle non-finite values.
Results may differ from a plain program's by a relative error of at most 0.0061.
Values may be sent and summed in bfloat16 or wider, within the bound.
A program may use at most 128 MiB of HBM per device.

v0:
```python
import math
import jax
import jax.numpy as jnp
from jax import lax
from jax.sharding import PartitionSpec as P

H = 8
E = 64


def attend(query_block, grad_block, key_image, value_image, weight):
    scale = 1.0 / math.sqrt(E)
    scores = (
        jnp.einsum("lhe,phe->lhp", query_block, key_image, preferred_element_type=jnp.float32)
        * scale
    )
    probs = jax.nn.softmax(scores, axis=-1)
    dprobs = jnp.einsum("lhe,phe->lhp", grad_block, value_image, preferred_element_type=jnp.float32)
    delta = jnp.sum(probs * dprobs, axis=-1, keepdims=True)
    masked = (probs * weight).astype(jnp.bfloat16)
    dscores = (weight * probs * (dprobs - delta) * scale).astype(jnp.bfloat16)
    query_grad = jnp.einsum("lhp,phe->lhe", dscores, key_image, preferred_element_type=jnp.float32)
    return (masked, dscores, query_grad)


def body(queries, keys, values, grad_out, block_mask):
    lab_rows, feature_width = queries.shape
    blocks = block_mask.shape[0]
    img_count = keys.shape[0]
    block_rows = lab_rows // blocks
    keys_full, values_full = (
        lax.all_gather(keys, "lab", axis=1, tiled=True),
        lax.all_gather(values, "lab", axis=1, tiled=True),
    )
    patches = keys_full.shape[1]
    query_blocks = queries.reshape(blocks, block_rows, H, E)
    grad_blocks = grad_out.reshape(img_count, blocks, block_rows, H, E)
    weights = block_mask.astype(jnp.float32)
    key_image = keys_full[0].reshape(patches, H, E)
    value_image = values_full[0].reshape(patches, H, E)

    def run_block(carry, pieces):
        query_block, grad_block, weight = pieces
        masked, dscores, query_grad = attend(
            query_block, grad_block, key_image, value_image, weight
        )
        dk_acc, dv_acc = carry
        dk_acc = dk_acc + jnp.einsum(
            "lhp,lhe->phe", dscores, query_block, preferred_element_type=jnp.float32
        )
        dv_acc = dv_acc + jnp.einsum(
            "lhp,lhe->phe", masked, grad_block, preferred_element_type=jnp.float32
        )
        return ((dk_acc, dv_acc), query_grad)

    zero_acc = jnp.zeros((patches, H, E), jnp.float32)
    (dk_acc, dv_acc), query_grads = lax.scan(
        run_block, (zero_acc, zero_acc), (query_blocks, grad_blocks[0], weights[:, 0])
    )
    key_terms = [dk_acc.reshape(patches, feature_width)]
    value_terms = [dv_acc.reshape(patches, feature_width)]
    key_stack = jnp.stack(key_terms)
    value_stack = jnp.stack(value_terms)
    key_sum = lax.psum_scatter(key_stack, "lab", scatter_dimension=1, tiled=True)
    value_sum = lax.psum_scatter(value_stack, "lab", scatter_dimension=1, tiled=True)
    grad_keys = key_sum.astype(jnp.bfloat16)
    grad_values = value_sum.astype(jnp.bfloat16)
    summed = lax.psum_scatter(
        query_grads.reshape(lab_rows, feature_width), "img", scatter_dimension=0, tiled=True
    )
    grad_queries = summed.astype(jnp.bfloat16)
    return (grad_queries, grad_keys, grad_values)


def solution(mesh):
    return jax.shard_map(
        body,
        mesh=mesh,
        in_specs=(
            P("lab", None),
            P("img", "lab", None),
            P("img", "lab", None),
            P("img", "lab", None),
            P("lab", "img"),
        ),
        out_specs=(P(("lab", "img"), None), P("img", "lab", None), P("img", "lab", None)),
        check_vma=False,
    )
```

profile of v0, /device:TPU:1, one launch (start us, length us, event | category | flops | bytes accessed | tf_op | source)
XLA Modules:
  0.0 575.3 jit_solution(8856966647616170280)
XLA Ops:
  7.2 2.9 reshape.17
  10.1 1.9 copy.43
  13.2 1.9 copy.44
  15.1 49.2 %all_gather.6 = bf16[1,576,512]{2,0,1:T(2,128)(2,1)S(1)} all-gather(bf16[1,18,512]{2,0,1:T(2,128)(2,1)S(1)} %copy.38), channel_id=1, replica_groups=mesh['lab'=32,'img'=16] {'lab'}, dimensions={1}, use_global_device_ids=true | all-gather | bytes 608256 | tf_op jit(solution)/shard_map/all_gather | solution.py:32
  64.3 2.5 copy.39
  66.8 41.1 %all_gather.7 = bf16[1,576,512]{2,0,1:T(2,128)(2,1)S(1)} all-gather(bf16[1,18,512]{2,0,1:T(2,128)(2,1)S(1)} %copy.41), channel_id=1, replica_groups=mesh['lab'=32,'img'=16] {'lab'}, dimensions={1}, use_global_device_ids=true | all-gather | bytes 608256 | tf_op jit(solution)/shard_map/all_gather | solution.py:33
  107.9 1.6 copy.42
  109.5 162.1 %while.15 = (s32[]{:T(128)}, f32[576,8,64]{0,2,1:T(8,128)}, f32[576,8,64]{0,2,1:T(8,128)}, f32[8,128,8,64]{1,3,2,0:T(8,128)}, bf16[8,128,8,64]{1,3,2,0:T(8,128)(...) while((s32[]{:T(128)}, f32[576,8,64]{0,2,1:T(8,128)}, ...), condition=%wide.region_4.5_spmd.clone, body=%wide.region_0.4_spmd.clone.sunk | while | flops 391646912 | bytes 33648772 | solution.py:57
  109.5 3.6 fusion.79
  115.1 4.9 fusion.82
  120.0 4.0 fusion.81
  124.0 5.1 fusion.80
  129.1 3.6 fusion.79
  132.7 1.5 fusion.78
  134.8 4.9 fusion.82
  139.6 4.4 fusion.81
  144.0 5.5 fusion.80
  149.5 3.6 fusion.79
  155.1 4.9 fusion.82
  160.0 4.4 fusion.81
  164.4 5.5 fusion.80
  169.8 3.6 fusion.79
  175.5 4.9 fusion.82
  180.3 4.4 fusion.81
  184.7 5.5 fusion.80
  190.2 3.6 fusion.79
  193.8 1.5 fusion.78
  195.8 4.9 fusion.82
  200.7 4.4 fusion.81
  205.1 5.5 fusion.80
  210.5 3.6 fusion.79
  214.1 1.5 fusion.78
  216.2 4.9 fusion.82
  221.0 4.4 fusion.81
  225.4 5.5 fusion.80
  230.9 3.6 fusion.79
  236.5 4.8 fusion.82
  241.4 4.4 fusion.81
  245.7 5.5 fusion.80
  251.2 3.6 fusion.79
  256.9 4.9 fusion.82
  261.7 4.4 fusion.81
  266.1 5.5 fusion.80
  271.6 3.9 copy.57
  275.4 4.8 reshape.19
  282.8 2.9 copy.47
  287.6 247.9 %all-reduce.4 = (bf16[1,576,512]{2,0,1:T(2,128)(2,1)S(1)}, bf16[1,576,512]{2,0,1:T(2,128)(2,1)}) all-reduce(f32[1,576,512]{2,0,1:T(1,128)S(1)} %copy.46, f32[1,576,512]{2,0,1:T(1,128)S(1)} %copy.47), channel_id=3, replica_groups=mesh['lab'=32,'img'=16] {'lab'}, use_global_device_ids=true, to_apply=%region_6.7.clone | all-reduce | flops 589824 | bytes 3538944
  537.5 29.2 %reduce-scatter.4.cloned.1.call-done = f32[64,512]{1,0:T(8,128)} async-done(((f32[1024,512]{1,0:T(8,128)}), f32[64,512]{1,0:T(8,128)}) %reduce-scatter.4.cloned.1.call-update) | async-done | bytes 131088
  (39 shorter events, 20.9 us)
Async XLA Ops:
  7.2 559.5 %reduce-scatter.4.cloned.1.call-start = ((), (), s32[]{:S(2)}) async-start(), calls=%async_computation.1 | async-start | bytes 2228224
  7.2 4.8 copy-start.1
  12.1 3.0 copy-start.2
  13.2 53.6 %copy-start.3 = (bf16[1,18,512]{2,1,0:T(8,128)(2,1)S(1)}, bf16[1,18,512]{2,1,0:T(8,128)(2,1)}, u32[]{:S(2)}) copy-start(bf16[1,18,512]{2,1,0:T(8,128)(2,1)} %param.9) | copy-start | bytes 55300
  64.3 45.2 %copy-start.4 = (s32[8,1]{0,1:T(1,128)S(1)}, s32[8,1]{0,1:T(1,128)}, u32[]{:S(2)}) copy-start(s32[8,1]{0,1:T(1,128)} %param.11) | copy-start | bytes 100
  280.2 1.3 copy-start
Sparse Core Ops, SparseCore 0:
  280.3 286.3 reduce-scatter.3
where the time goes:
time: 576 us; the launch traced here: 575 us
  blocking collectives  338 us (59%)
  matrix products  157 us (27%)
  local copies, waits for them, and re-layouts  35.8 us (6%)
  waiting for transfers between devices  29.2 us (5%)
  between operations  14.8 us (3%)
    unnamed x1, blocking collectives  248 us
    all_gather x1, blocking collectives, body(): lax.all_gather(keys, 'lab', axis=1, tiled=True)  49.2 us
    dot_general x8, matrix products, run_block(): jnp.einsum('lhp,lhe->phe', dscores, query_block, preferred_element_type=j...  43.4 us
    all_gather x1, blocking collectives, body(): lax.all_gather(values, 'lab', axis=1, tiled=True)  41.1 us
    dot_general x8, matrix products, attend(): jnp.einsum('lhp,phe->lhe', dscores, key_image, preferred_element_type=jnp...  38.9 us
    dot_general x8, matrix products, run_block(): jnp.einsum('lhp,lhe->phe', masked, grad_block, preferred_element_type=jnp...  34.7 us
    unnamed x2, waiting for transfers between devices  29.2 us
    sub x8, matrix products, attend(): probs = jax.nn.softmax(scores, axis=-1)  28.7 us
  transfers between devices with their start and end apart: 1, of which 1 were waited for; matrix products, arithmetic and copies ran while one was open for 1% of the time, Pallas kernels for 0%

commit v1 on v0

--- a/solution.py
+++ b/solution.py
@@ -6,6 +6,11 @@
 
 H = 8
 E = 64
+
+
+def swapped_in(x, mesh_axis, along):
+    sent = jnp.stack([x] * lax.axis_size(mesh_axis))
+    return jnp.concatenate(lax.all_to_all(sent, mesh_axis, 0, 0), axis=along)
 
 
 def attend(query_block, grad_block, key_image, value_image, weight):
@@ -29,7 +34,7 @@
     img_count = keys.shape[0]
     block_rows = lab_rows // blocks
     keys_full, values_full = (
-        lax.all_gather(keys, "lab", axis=1, tiled=True),
+        swapped_in(keys, "lab", 1),
         lax.all_gather(values, "lab", axis=1, tiled=True),
     )
     patches = keys_full.shape[1]

time: 576 us -> 549 us (0.953)
  blocking collectives: 338 us -> 295 us
  starting transfers between devices: 0.04 us -> 10.5 us
    all_gather x1 -> x0, blocking collectives: 49.2 us -> none  [body(): lax.all_gather(keys, 'lab', axis=1, tiled=True)]
    all_to_all x0 -> x1, starting transfers between devices: none -> 10.4 us  [swapped_in(): return jnp.concatenate(lax.all_to_all(sent, mesh_axis, 0, 0), axis=along)]
    unnamed x21 -> x17, local copies, waits for them, and re-layouts: 18.1 us -> 18.7 us
  transfers between devices with their start and end apart: 1 -> 2, of which waited for: 1 -> 1; matrix products, arithmetic and copies ran while one was open for 1% -> 3% of each run, Pallas kernels for 0% -> 0%
where the time goes in v1:
time: 549 us; the launch traced here: 547 us
  blocking collectives  295 us (54%)
  matrix products  157 us (29%)
  local copies, waits for them, and re-layouts  37.9 us (7%)
  waiting for transfers between devices  32.1 us (6%)
  between operations  14.8 us (3%)
  starting transfers between devices  10.5 us (2%)
    unnamed x1, blocking collectives  248 us
    all_gather x1, blocking collectives, body(): lax.all_gather(values, 'lab', axis=1, tiled=True)  46.7 us
    dot_general x8, matrix products, run_block(): jnp.einsum('lhp,lhe->phe', dscores, query_block, preferred_element_type=j...  43.4 us
    dot_general x8, matrix products, attend(): jnp.einsum('lhp,phe->lhe', dscores, key_image, preferred_element_type=jnp...  38.9 us
    dot_general x8, matrix products, run_block(): jnp.einsum('lhp,lhe->phe', masked, grad_block, preferred_element_type=jnp...  34.7 us
    unnamed x2, waiting for transfers between devices  32.1 us
    sub x8, matrix products, attend(): probs = jax.nn.softmax(scores, axis=-1)  28.7 us
    unnamed x17, local copies, waits for them, and re-layouts  18.7 us
  transfers between devices with their start and end apart: 2, of which 1 were waited for; matrix products, arithmetic and copies ran while one was open for 3% of the time, Pallas kernels for 0%

profile of v1, /device:TPU:1, one launch (start us, length us, event | category | flops | bytes accessed | tf_op | source)
XLA Modules:
  0.0 547.3 jit_solution(9081872651115239589)
XLA Ops:
  7.2 1.7 stack.2
  8.9 10.4 %all-to-all-start = ((bf16[32,1,18,512]{3,2,1,0:T(8,128)(2,1)}), bf16[32,1,18,512]{3,2,1,0:T(8,128)(2,1)S(1)}, u32[]{:S(2)}, u32[]{:S(2)}) async-start(bf16[32,1,18,512]{3,2,1,0:T(8,128)(2,1)} %stack.2), calls=%async_computation | async-start | bytes 1572864 | tf_op jit(solution)/shard_map/all_to_all | solution.py:13
  19.4 2.8 reshape.20
  22.2 1.9 copy.40
  24.1 2.8 reshape.21
  26.9 1.9 copy.42
  28.9 46.7 %all_gather.3 = bf16[1,576,512]{2,0,1:T(2,128)(2,1)S(1)} all-gather(bf16[1,18,512]{2,0,1:T(2,128)(2,1)S(1)} %copy.38), channel_id=1, replica_groups=mesh['lab'=32,'img'=16] {'lab'}, dimensions={1}, use_global_device_ids=true | all-gather | bytes 608256 | tf_op jit(solution)/shard_map/all_gather | solution.py:38
  75.6 1.6 copy.39
  77.8 1.8 copy.41
  79.7 162.1 %while.15 = (s32[]{:T(128)}, f32[576,8,64]{0,2,1:T(8,128)}, f32[576,8,64]{0,2,1:T(8,128)}, f32[8,128,8,64]{1,3,2,0:T(8,128)}, bf16[8,128,8,64]{1,3,2,0:T(8,128)(...) while((s32[]{:T(128)}, f32[576,8,64]{0,2,1:T(8,128)}, ...), condition=%wide.region_4.5_spmd.clone, body=%wide.region_0.4_spmd.clone.sunk | while | flops 391646912 | bytes 33648772 | solution.py:62
  79.7 3.6 fusion.79
  83.3 1.5 fusion.78
  85.3 4.9 fusion.82
  90.2 4.0 fusion.81
  94.2 5.1 fusion.80
  99.3 3.6 fusion.79
  105.0 4.9 fusion.82
  109.8 4.4 fusion.81
  114.2 5.5 fusion.80
  119.7 3.6 fusion.79
  125.3 4.9 fusion.82
  130.2 4.4 fusion.81
  134.6 5.5 fusion.80
  140.0 3.6 fusion.79
  145.7 4.9 fusion.82
  150.5 4.4 fusion.81
  154.9 5.5 fusion.80
  160.4 3.6 fusion.79
  166.0 4.9 fusion.82
  170.9 4.4 fusion.81
  175.3 5.5 fusion.80
  180.7 3.6 fusion.79
  186.4 4.9 fusion.82
  191.2 4.4 fusion.81
  195.6 5.5 fusion.80
  201.1 3.6 fusion.79
  206.7 4.8 fusion.82
  211.6 4.4 fusion.81
  215.9 5.5 fusion.80
  221.4 3.6 fusion.79
  227.0 4.9 fusion.82
  231.9 4.4 fusion.81
  236.3 5.5 fusion.80
  241.8 3.9 copy.55
  245.6 4.8 reshape.22
  253.7 2.9 copy.45
  256.6 247.9 %all-reduce.4 = (bf16[1,576,512]{2,0,1:T(2,128)(2,1)S(1)}, bf16[1,576,512]{2,0,1:T(2,128)(2,1)}) all-reduce(f32[1,576,512]{2,0,1:T(1,128)S(1)} %copy.44, f32[1,576,512]{2,0,1:T(1,128)S(1)} %copy.45), channel_id=3, replica_groups=mesh['lab'=32,'img'=16] {'lab'}, use_global_device_ids=true, to_apply=%region_6.7.clone | all-reduce | flops 589824 | bytes 3538944
  506.6 32.1 %reduce-scatter.4.cloned.1.call-done = f32[64,512]{1,0:T(8,128)} async-done(((f32[1024,512]{1,0:T(8,128)}), f32[64,512]{1,0:T(8,128)}) %reduce-scatter.4.cloned.1.call-update) | async-done | bytes 131088
  (37 shorter events, 22.2 us)
Async XLA Ops:
  8.9 68.3 %all-to-all-start = ((bf16[32,1,18,512]{3,2,1,0:T(8,128)(2,1)}), bf16[32,1,18,512]{3,2,1,0:T(8,128)(2,1)S(1)}, u32[]{:S(2)}, u32[]{:S(2)}) async-start(bf16[32,1,18,512]{3,2,1,0:T(8,128)(2,1)} %stack.2), calls=%async_computation | async-start | bytes 1572864 | tf_op jit(solution)/shard_map/all_to_all | solution.py:13
  19.3 519.4 %reduce-scatter.4.cloned.1.call-start = ((), (), s32[]{:S(2)}) async-start(), calls=%async_computation.2 | async-start | bytes 2228224
  24.1 4.7 copy-start.1
  26.9 50.3 %copy-start.2 = (s32[8,1]{0,1:T(1,128)S(1)}, s32[8,1]{0,1:T(1,128)}, u32[]{:S(2)}) copy-start(s32[8,1]{0,1:T(1,128)} %param.11) | copy-start | bytes 100
  250.4 2.1 copy-start
Sparse Core Ops, SparseCore 0:
  250.5 288.0 reduce-scatter.3
